TPU v7x, 512 devices: a whole 4x8x8 slice. The times are simulated.
512 devices in a mesh: dp: 8 (over x, core), shard: 64 (over y, z).
Axes of the slice: x: 4, y: 8, z: 8, core: 2. Of those that a mesh axis runs over, the one named last changes fastest.
Arguments:
- queries: bfloat16 [262144, 1024], P(('dp', 'shard')), may hold values from -6 to 6
- query_weight: bfloat16 [1024, 256], replicated, may hold values from -0.1875 to 0.1875
- item_weight: bfloat16 [1024, 256], replicated, may hold values from -0.1875 to 0.1875
- table: bfloat16 [16384, 1024], P('shard'), may hold values from -6 to 6
- queue: bfloat16 [65536, 256], P(('dp', 'shard')), may hold values from -0.0625 to 0.0625
- requests: int32 [32768, 4], P(('dp', 'shard')), may hold values from -1 to 255, as said below
- inverse: int32 [262144], P(('dp', 'shard')), may hold values from 0 to 255, as said below
- write_owner: int32 [1], replicated, may hold values from 0 to 63
Outputs:
- query_update: bfloat16 [1024, 256], replicated
- item_update: bfloat16 [1024, 256], replicated
- new_queue: bfloat16 [65536, 256], P(('dp', 'shard'))
Inputs may be any that keep to these rules, and one draw needn't show every extreme that they name: `requests`: in each block an entry is a local row of the owner or -1; entries at and after the block's count are -1, at least one is not; the rows of one block are distinct; every device has a block with exactly 4 rows. `inverse`: every entry names a slot o * 4 + c whose request entry is not -1; every such slot of the device is named by some query.
All inputs are finite; a program needn't handle non-finite values.
Results may differ from a plain program's by a relative error of at most 0.015.
Values may be sent and summed in bfloat16 or wider, within the bound.
A program may use at most 64 MiB of HBM per device.

v0:
```python
import math

import jax
import jax.numpy as jnp
from jax import lax
from jax.sharding import PartitionSpec as P

FRESH_DEV = 1


LOGIT_SCALE = 50.0
NORM_EPS = 1e-06


def unit_rows(raw_rows):
    sq_total = jnp.sum(raw_rows * raw_rows, axis=-1, keepdims=True) + NORM_EPS
    return (raw_rows * lax.rsqrt(sq_total), sq_total)


def unit_back(raw_rows, sq_total, grad_in):
    inner_dot = jnp.sum(raw_rows * grad_in, axis=-1, keepdims=True)
    root_inv = lax.rsqrt(sq_total)
    return grad_in * root_inv - raw_rows * (inner_dot * root_inv / sq_total)


def per_device(queries, query_weight, item_weight, table, queue, requests, inverse, write_owner):
    model_width, embed_width = query_weight.shape
    slot_count = requests.shape[0] * requests.shape[1]
    looked = table[
        jnp.maximum(lax.all_to_all(requests, "shard", split_axis=0, concat_axis=0, tiled=True), 0)
    ]
    received = lax.all_to_all(looked, "shard", split_axis=0, concat_axis=0, tiled=True)
    fetched = received.reshape(slot_count, model_width)
    item_raw = jnp.dot(fetched, item_weight, preferred_element_type=jnp.float32).astype(
        jnp.bfloat16
    )
    item_wide = item_raw.astype(jnp.float32)
    item_unit, item_total = unit_rows(item_wide)
    item_embed = item_unit.astype(jnp.bfloat16)
    query_raw = jnp.dot(queries, query_weight, preferred_element_type=jnp.float32)
    query_unit, query_total = unit_rows(query_raw)
    query_embed = query_unit.astype(jnp.bfloat16)
    positive = item_embed[inverse]
    pos_logit = LOGIT_SCALE * jnp.sum(
        query_embed.astype(jnp.float32) * positive.astype(jnp.float32), axis=1
    )
    shard_piece = lax.all_gather(queue, "shard", axis=0, tiled=True)
    neg_logit = LOGIT_SCALE * jnp.einsum(
        "qe,ne->qn", query_embed, shard_piece, preferred_element_type=jnp.float32
    )
    expos = jnp.exp(neg_logit)
    weighted = jnp.dot(expos.astype(jnp.bfloat16), shard_piece, preferred_element_type=jnp.float32)
    expo_sum, weighted = (jnp.sum(expos, axis=1), weighted)
    pos_expo = jnp.exp(pos_logit)
    denom = pos_expo + expo_sum
    pos_share = pos_expo / denom
    query_grad = LOGIT_SCALE * (
        weighted / denom[:, None] + (pos_share - 1.0)[:, None] * positive.astype(jnp.float32)
    )
    pos_grad = LOGIT_SCALE * (pos_share - 1.0)[:, None] * query_embed.astype(jnp.float32)
    one_hot = (inverse[:, None] == jnp.arange(slot_count, dtype=jnp.int32)[None, :]).astype(
        jnp.float32
    )
    item_grad = jnp.einsum("qs,qe->se", one_hot, pos_grad, precision=lax.Precision.HIGHEST)
    query_back = unit_back(query_raw, query_total, query_grad).astype(jnp.bfloat16)
    item_back = unit_back(item_wide, item_total, item_grad).astype(jnp.bfloat16)
    fresh_embed = positive[:FRESH_DEV]
    all_fresh = lax.all_gather(fresh_embed, "shard", axis=0, tiled=True)
    updated = lax.dynamic_update_slice_in_dim(queue, all_fresh, 0, 0)
    is_owner = lax.axis_index("shard") == write_owner[0]
    new_queue = jnp.where(is_owner, updated, queue)
    clip_limit = math.sqrt(2.0 * model_width * embed_width)
    query_term = jnp.einsum("qd,qe->de", queries, query_back, preferred_element_type=jnp.float32)
    item_term = jnp.einsum("qd,qe->de", fetched, item_back, preferred_element_type=jnp.float32)
    query_sum, item_sum = lax.psum((query_term, item_term), ("dp", "shard"))
    squares = jnp.sum(query_sum * query_sum) + jnp.sum(item_sum * item_sum)
    factor = jnp.minimum(1.0, clip_limit / jnp.sqrt(squares + NORM_EPS))
    return (
        (query_sum * factor).astype(jnp.bfloat16),
        (item_sum * factor).astype(jnp.bfloat16),
        new_queue,
    )


def solution(mesh):
    placed = (
        P(("dp", "shard"), None),
        P(),
        P(),
        P("shard", None),
        P(("dp", "shard"), None),
        P(("dp", "shard"), None),
        P(("dp", "shard")),
        P(),
    )
    return jax.shard_map(
        per_device,
        mesh=mesh,
        in_specs=placed,
        out_specs=(P(), P(), P(("dp", "shard"), None)),
        check_vma=False,
    )
```

profile of v0, /device:TPU:1, one launch (start us, length us, event | category | flops | bytes accessed | tf_op | source)
XLA Modules:
  0.0 424.2 jit_solution(1345117881275761527)
XLA Ops:
  7.2 0.0 copy-start
  7.2 0.0 all-gather.3.cloned.1.call-start
  7.2 1.6 copy.42
  8.8 0.0 all-gather.3.cloned.1.call-update
  8.8 0.8 copy.28
  9.6 27.8 %all_to_all.14 = s32[64,1,4]{2,1,0:T(1,128)S(1)} all-to-all(s32[64,1,4]{2,1,0:T(1,128)S(1)} %bitcast.20), channel_id=1, replica_groups=mesh['dp'=8,'shard'=64] {'shard'}, dimensions={0} | all-to-all | bytes 2048 | tf_op jit(solution)/shard_map/all_to_all | solution.py:30
  37.3 0.1 maximum_reduce_fusion
  37.4 0.1 reshape.74
  37.6 2.7 gather_fusion
  40.2 0.0 copy-start.4
  40.3 1.0 reshape.73
  41.2 4.6 %all-to-all-start.1 = ((bf16[64,4,1024]{2,1,0:T(4,128)(2,1)}), bf16[64,4,1024]{2,1,0:T(4,128)(2,1)S(1)}, u32[]{:S(2)}, u32[]{:S(2)}) async-start(bf16[64,4,1024]{2,1,0:T(4,128)(2,1)} %reshape.73), calls=%async_computation.1 | async-start | bytes 1048576 | tf_op jit(solution)/shard_map/all_to_all | solution.py:32
  45.9 0.0 all-reduce.3.cloned.1.call-start
  45.9 0.7 compare_select_fusion
  46.6 0.0 copy-done
  46.6 1.5 multiply_reduce_fusion.3
  48.2 14.5 %all-to-all-done.1 = bf16[64,4,1024]{2,1,0:T(4,128)(2,1)S(1)} async-done(((bf16[64,4,1024]{2,1,0:T(4,128)(2,1)}), bf16[64,4,1024]{2,1,0:T(4,128)(2,1)S(1)}, u32[]{:S(2)}, u32[]{:S(2)}) %all-to-all-start.1) | async-done | bytes 524320 | tf_op jit(solution)/shard_map/all_to_all | solution.py:32
  62.7 0.1 reshape.71
  62.8 1.4 multiply_reduce_fusion.5
  64.2 0.1 copy.29
  64.3 2.0 gather_fusion.1
  66.3 0.1 copy.30
  66.5 0.1 fusion.13
  66.6 39.5 %all-gather.3.cloned.1.call-done = bf16[8192,256]{1,0:T(8,128)(2,1)} async-done(((bf16[128,256]{1,0:T(8,128)(2,1)}), bf16[8192,256]{1,0:T(8,128)(2,1)}) %all-gather.3.cloned.1.call-update) | async-done | bytes 4194320 | tf_op jit(solution)/shard_map/all_gather | solution.py:47
  106.1 0.0 copy-start.1
  106.1 9.7 %fusion = (f32[512]{0:T(512)S(1)}, f32[512,8192]{1,0:T(8,128)}) fusion(bf16[512,256]{0,1:T(8,128)(2,1)S(1)} %get-tuple-element.20, bf16[8192,256]{1,0:T(8,128)(2,1)} %all-gather.3.cloned.1.call-done), kind=kOutput, calls=%fused_computation.3 | convolution fusion | flops 2155871744 | bytes 21235712 | tf_op jit(solution)/shard_map/qe,ne->qn/dot_general | solution.py:48
  115.8 0.0 copy-done.4
  115.8 0.5 multiply_reduce_fusion.4
  116.4 0.0 copy-done.1
  116.4 0.0 copy-start.2
  116.4 8.0 %multiply_reduce_fusion.2 = (f32[512]{0:T(512)S(1)}, f32[512,256]{0,1:T(8,128)S(1)}) fusion(f32[512,256]{0,1:T(8,128)S(1)} %get-tuple-element.27, bf16[512,256]{0,1:T(8,128)(2,1)S(1)} %copy.30, f32[512]{0:T(512)S(1)} %get-tuple-element.18, f32[512]{0:T(512)S(1)} %get-tuple-element.21, bf16[8192,256]{1,0:T(8,128)(2,1)S(1)} %copy-done.1, ...), kind=kOutput, calls=%fused_computation.23 | convolution fusion | flops 2156789248 | bytes 22288384 | tf_op jit(solution)/shard_map/dot_general | solution.py:52
  124.4 1.3 fusion.18
  125.7 1.4 convolution_bitcast_fusion
  127.1 0.0 all-reduce.3.cloned.1.call-update
  127.8 36.8 %all-gather = bf16[64,1,256]{2,1,0:T(2,128)(2,1)S(1)} all-gather(bf16[1,1,256]{2,1,0:T(2,128)(2,1)S(1)} %slice_bitcast_fusion), channel_id=1, replica_groups=mesh['dp'=8,'shard'=64] {'shard'}, dimensions={0}, use_global_device_ids=true | all-gather | bytes 33280 | tf_op jit(solution)/shard_map/all_gather | solution.py:68
  164.6 0.0 copy-done.2
  164.7 0.0 copy-start.3
  164.7 243.3 %all-reduce.3.cloned.1.call-done = (f32[1024,256]{0,1:T(8,128)}, f32[1024,256]{0,1:T(8,128)}) async-done(((f32[1024,256]{0,1:T(8,128)}, f32[1024,256]{0,1:T(8,128)}), (f32[1024,256]{0,1:T(8,128)}, f32[1024,256]{0,1:T(8,128)})) %all-reduce.3.cloned.1.call-update) | async-done | bytes 2097168 | tf_op jit(solution)/shard_map/psum | solution.py:75
  408.0 2.1 multiply_reduce_fusion
  410.1 2.1 multiply_reduce_fusion.1
  413.5 1.8 multiply_convert_fusion
  415.3 1.0 copy.33
  416.3 1.0 copy.32
  417.3 0.0 copy-done.3
  (10 shorter events, 0.1 us)
Async XLA Ops:
  7.2 39.5 %copy-start = (bf16[512,1024]{1,0:T(8,128)(2,1)S(1)}, bf16[512,1024]{1,0:T(8,128)(2,1)}, u32[]{:S(2)}) copy-start(bf16[512,1024]{1,0:T(8,128)(2,1)} %param.8) | copy-start | bytes 3145732
  7.2 98.9 %all-gather.3.cloned.1.call-start = ((), (), s32[]{:S(2)}) async-start(), calls=%async_computation.2 | async-start | bytes 4259840 | tf_op jit(solution)/shard_map/all_gather | solution.py:47
  40.2 75.6 %copy-start.4 = (s32[512]{0:T(512)S(1)}, s32[512]{0:T(512)}, u32[]{:S(2)}) copy-start(s32[512]{0:T(512)} %param.14) | copy-start | bytes 6148
  41.2 21.4 %all-to-all-start.1 = ((bf16[64,4,1024]{2,1,0:T(4,128)(2,1)}), bf16[64,4,1024]{2,1,0:T(4,128)(2,1)S(1)}, u32[]{:S(2)}, u32[]{:S(2)}) async-start(bf16[64,4,1024]{2,1,0:T(4,128)(2,1)} %reshape.73), calls=%async_computation.1 | async-start | bytes 1048576 | tf_op jit(solution)/shard_map/all_to_all | solution.py:32
  45.9 362.1 %all-reduce.3.cloned.1.call-start = ((), (), s32[]{:S(2)}) async-start(), calls=%async_computation.3 | async-start | bytes 4194304 | tf_op jit(solution)/shard_map/psum | solution.py:75
  106.1 10.3 %copy-start.1 = (bf16[8192,256]{1,0:T(8,128)(2,1)S(1)}, bf16[8192,256]{1,0:T(8,128)(2,1)}, u32[]{:S(2)}) copy-start(bf16[8192,256]{1,0:T(8,128)(2,1)} %all-gather.3.cloned.1.call-done) | copy-start | bytes 12582916
  116.4 48.3 %copy-start.2 = (bf16[128,256]{1,0:T(8,128)(2,1)S(1)}, bf16[128,256]{1,0:T(8,128)(2,1)}, u32[]{:S(2)}) copy-start(bf16[128,256]{1,0:T(8,128)(2,1)} %copy.42) | copy-start | bytes 196612
  164.7 252.7 %copy-start.3 = (bf16[128,256]{1,0:T(8,128)(2,1)}, bf16[128,256]{1,0:T(8,128)(2,1)S(1)}, u32[]{:S(2)}) copy-start(bf16[128,256]{1,0:T(8,128)(2,1)S(1)} %fusion.21) | copy-start | bytes 196612
Sparse Core Ops, SparseCore 0:
  11.6 94.4 all-gather.2
  127.3 280.6 all-reduce.2
where the time goes:
time: 425 us; the launch traced here: 424 us
  waiting for transfers between devices  297 us (70%)
  blocking collectives  64.6 us (15%)
  matrix products  23.9 us (6%)
  between operations  16.2 us (4%)
  local copies, waits for them, and re-layouts  10.4 us (2%)
  other arithmetic  6.97 us (2%)
  starting transfers between devices  4.71 us (1%)
    psum x1, waiting for transfers between devices, per_device(): query_sum, item_sum = lax.psum((query_term, item_term), ('dp', 'shard'))  243 us
    all_gather x1, waiting for transfers between devices, per_device(): shard_piece = lax.all_gather(queue, 'shard', axis=0, tiled=True)  39.5 us
    all_gather x1, blocking collectives, per_device(): all_fresh = lax.all_gather(fresh_embed, 'shard', axis=0, tiled=True)  36.8 us
    all_to_all x1, blocking collectives, per_device(): lax.all_to_all(requests, 'shard', split_axis=0, concat_axis=0, tiled=True)  27.8 us
    all_to_all x1, waiting for transfers between devices, per_device(): lax.all_to_all(looked, 'shard', split_axis=0, concat_axis=0, tiled=True)  14.5 us
    dot_general x1, matrix products, per_device(): jnp.einsum('qe,ne->qn', query_embed, shard_piece, preferred_element_type=...  9.7 us
  transfers between devices with their start and end apart: 3, of which 3 were waited for; matrix products, arithmetic and copies ran while one was open for 3% of the time, Pallas kernels for 0%

commit v1 on v0

v1 whole, which is shorter than its diff:
```python
import functools
import math

import jax
import jax.numpy as jnp
from jax import lax
from jax.experimental import pallas as pl
from jax.experimental.pallas import tpu as pltpu
from jax.sharding import PartitionSpec as P

SCALE = 50.0
EPS = 1e-06
CAP = 4
BF = jnp.bfloat16
F32 = jnp.float32
LOG2E = math.log2(math.e)
MESH = pl.DeviceIdType.MESH


def dot(a, b, lhs=1, rhs=0):
    return lax.dot_general(a, b, (((lhs,), (rhs,)), ((), ())), preferred_element_type=F32)


def split_dot(a, wide):
    high = wide.astype(BF)
    low = (wide - high.astype(F32)).astype(BF)
    return dot(a, high) + dot(a, low)


def pick(mask):
    return jnp.where(mask, 1.0, 0.0).astype(BF)


def unit_back(raw, total, grad):
    inner = jnp.sum(raw * grad, axis=-1, keepdims=True)
    inv = lax.rsqrt(total)
    return grad * inv - raw * (inner * inv / total)


class Sems:
    def __init__(self, send, recv):
        self.send, self.recv, self.used = send, recv, 0
        self.open = []

    def copy(self, src, dst, device):
        i = self.used
        self.used += 1
        made = pltpu.make_async_remote_copy(
            src_ref=src, dst_ref=dst, send_sem=self.send.at[i], recv_sem=self.recv.at[i],
            device_id=device, device_id_type=MESH,
        )
        self.open.append(made)
        return made


def n_sems(sizes):
    nx, ny, nz, nc = sizes
    y, z, x, c = ny - 1, nz - 1, nx - 1, nc - 1
    gather = y + z + 2 * (y + z)
    items = 2 * (y + z) * 2 + (y + z)
    reduce = 2 * (c + x + y) + z + y + x + c
    return gather + items + reduce


def kernel(sizes, q_ref, qw_ref, iw_ref, t_ref, r_ref, id_ref, inv_ref, outq_ref, outi_ref, fresh_ref,
           buf, qt, tt, traw, qraw, qe, wacc, dacc, mt, ot, iraw, pos,
           id1, id2, id2s, rs1, rr1, rs2, rr2, fs1, fr1, fs2, fr2, bs1, br1, bs2, br2,
           term, sc, rc, sx, rx, sy, ry, zs, rz, fin, send_sem, recv_sem):
    nx, ny, nz, nc = sizes
    ns = ny * nz
    slots = ns * CAP
    d, s = lax.axis_index("dp"), lax.axis_index("shard")
    x, core = lax.div(d, nc), lax.rem(d, nc)
    y, z = lax.div(s, nz), lax.rem(s, nz)
    at_y = lambda p: (d, p * nz + z)
    at_z = lambda p: (d, y * nz + p)
    at_x = lambda p: (p * nc + core, s)
    at_c = lambda p: (x * nc + p, s)
    sems = Sems(send_sem, recv_sem)

    barrier = pltpu.get_barrier_semaphore()
    total = 0
    for at, n, me in ((at_y, ny, y), (at_z, nz, z), (at_x, nx, x), (at_c, nc, core)):
        for k in range(1, n):
            pl.semaphore_signal(barrier, inc=1, device_id=at(lax.rem(me + k, n)), device_id_type=MESH)
            total += 1
    pl.semaphore_wait(barrier, total)

    def exchange(at, n, me, src, dst):
        made = []
        for k in range(1, n):
            p = lax.rem(me + k, n)
            made.append(sems.copy(src(p), dst(me), at(p)))
        for one in made:
            one.start()
        return made

    def arrive(made):
        for one in made:
            one.wait_recv()

    ids_y = exchange(at_y, ny, y, lambda p: id_ref.at[pl.ds(pl.multiple_of(p * nz, nz), nz)], lambda me: id1.at[me])
    half = r_ref.shape[0] // 2
    gather_y = exchange(at_y, ny, y, lambda p: r_ref.at[pl.ds(0, half)], lambda me: buf.at[0, z, me])
    gather_z = exchange(at_z, nz, z, lambda p: r_ref.at[pl.ds(half, half)], lambda me: buf.at[1, y, me])
    id1[y] = id_ref[pl.ds(pl.multiple_of(y * nz, nz), nz), :]
    buf[0, z, y] = r_ref[pl.ds(0, half), :]
    buf[1, y, z] = r_ref[pl.ds(half, half), :]

    traw[...] = dot(t_ref[...], iw_ref[...]).astype(BF)
    raw = dot(q_ref[...], qw_ref[...])
    qraw[...] = raw
    q_total = jnp.sum(raw * raw, axis=-1, keepdims=True) + EPS
    qe[...] = (raw * lax.rsqrt(q_total)).astype(BF)
    wacc[...] = jnp.zeros_like(wacc)
    dacc[...] = jnp.zeros_like(dacc)

    arrive(ids_y)
    id2s[...] = jnp.sum(id1[...], axis=0)
    id2[z] = id2s[...]
    ids_z = exchange(at_z, nz, z, lambda p: id2s, lambda me: id2.at[me])

    arrive(gather_y)
    arrive(gather_z)
    rings = ((at_z, nz, z, ny), (at_y, ny, y, nz))
    messages = {}
    for h, (at, n, me, width) in enumerate(rings):
        for left in (0, 1):
            for i in range(n - 1):
                last = i == n - 2
                away = n // 2 - 1 if last else i // 2
                part = left if last else i % 2
                col = lax.rem(me + (away if left else n - away), n)
                ref = buf.at[h, col, pl.ds(part * (width // 2), width // 2)]
                to = lax.rem(me + (n - 1 if left else 1), n)
                messages[h, left, i] = sems.copy(ref, ref, at(to))

    def go(h, left, i):
        messages[h, left, i].start()

    def attend(h, col, part, width):
        rows = buf[h, col, pl.ds(part * (width // 2), width // 2)]
        keys = rows.reshape(rows.shape[0] * rows.shape[1], rows.shape[2])
        expo = jnp.exp2(dot(qe[...], keys, 1, 1) * (SCALE * LOG2E))
        wacc[...] += dot(expo.astype(BF), keys)
        lanes = dacc.shape[1]
        dacc[...] += sum(expo[:, k : k + lanes] for k in range(0, expo.shape[1], lanes))

    def step(m):
        n = nz
        for h in (0, 1):
            for left in (0, 1):
                messages[h, left, m].wait_recv()
                last = n - 2
                if left and m == n - 3:
                    go(h, left, last)
                elif m + 2 <= last - left:
                    go(h, left, m + 2)

        def body(t, carry):
            h, left = lax.div(t, 2), lax.rem(t, 2)
            me = jnp.where(h == 0, z, y)
            away = m // 2 + 1
            col = lax.rem(jnp.where(left == 1, me + away, me + n - away), n)
            part = left if m == n - 2 else m % 2
            attend(h, col, part, n)
            return carry

        lax.fori_loop(0, 4, body, 0)

    for h in (0, 1):
        for left in (0, 1):
            for i in range(min(2, nz - 1)):
                go(h, left, i)

    arrive(ids_z)
    mine = lax.broadcasted_iota(jnp.int32, (nz, slots), 0) == z
    asked = jnp.sum(jnp.where(mine, jnp.sum(id2[...], axis=0), 0), axis=0, keepdims=True)
    mt[...] = pick(lax.broadcasted_iota(jnp.int32, mt.shape, 0) == asked)
    rs1[...] = dot(mt[...], traw[...], 0, 0).astype(BF).reshape(rs1.shape)
    rr1[y] = rs1[y]
    rows_y = exchange(at_y, ny, y, lambda p: rs1.at[p], lambda me: rr1.at[me])

    def own_body(t, carry):
        h = lax.div(t, 2)
        attend(h, jnp.where(h == 0, z, y), lax.rem(t, 2), nz)
        return carry

    lax.fori_loop(0, 4, own_body, 0)
    qt[...] = q_ref[...].T
    if nz - 1 > 0:
        step(0)

    def slot_of(i):
        zo, yo, c = i // (ny * CAP), (i // CAP) % ny, i % CAP
        return (yo * nz + zo) * CAP + c

    square = (slots, slots)
    arrive(rows_y)
    order = pick(lax.broadcasted_iota(jnp.int32, square, 1) == slot_of(lax.broadcasted_iota(jnp.int32, square, 0)))
    rs2[...] = dot(order, rr1[...].reshape(slots, -1)).astype(BF).reshape(rs2.shape)
    rr2[z] = rs2[z]
    rows_z = exchange(at_z, nz, z, lambda p: rs2.at[p], lambda me: rr2.at[me])
    tt[...] = t_ref[...].T
    for m in range(1, min(3, nz - 1)):
        step(m)

    arrive(rows_z)
    item = rr2[...].reshape(slots, -1).astype(F32)
    iraw[...] = item
    i_total = jnp.sum(item * item, axis=-1, keepdims=True) + EPS
    embed = (item * lax.rsqrt(i_total)).astype(BF)
    slot_rows = slot_of(lax.broadcasted_iota(jnp.int32, ot.shape, 0))
    ot[...] = pick(slot_rows == inv_ref[...])
    pos[...] = dot(ot[...], embed, 0, 0)
    first = jnp.broadcast_to(pos[0:1, :], fs1.shape)
    fs1[...] = jnp.where(lax.broadcasted_iota(jnp.int32, fs1.shape, 0) == y, first, 0.0).astype(BF)
    fr1[y] = fs1[...]
    fresh_y = exchange(at_y, ny, y, lambda p: fs1, lambda me: fr1.at[me])
    for m in range(3, min(5, nz - 1)):
        step(m)
    arrive(fresh_y)
    fs2[...] = jnp.sum(fr1[...].astype(F32), axis=0).astype(BF)
    fr2[z] = fs2[...]
    fresh_z = exchange(at_z, nz, z, lambda p: fs2, lambda me: fr2.at[me])
    for m in range(5, nz - 1):
        step(m)
    arrive(fresh_z)
    fshape = (ns, nz * fs2.shape[0])
    want = lax.broadcasted_iota(jnp.int32, fshape, 0)
    place = (want % nz) * fs2.shape[0] + want // nz
    fresh_ref[...] = dot(pick(lax.broadcasted_iota(jnp.int32, fshape, 1) == place),
                         fr2[...].reshape(fshape[1], -1)).astype(BF)

    raw = qraw[...]
    q_total = jnp.sum(raw * raw, axis=-1, keepdims=True) + EPS
    embed = qe[...].astype(F32)
    positive = pos[...]
    pos_expo = jnp.exp(SCALE * jnp.sum(embed * positive, axis=1, keepdims=True))
    denom = pos_expo + jnp.sum(dacc[...], axis=1, keepdims=True)
    less = pos_expo / denom - 1.0
    item_grad = split_dot(ot[...], (SCALE * less) * embed)
    item = iraw[...]
    i_total = jnp.sum(item * item, axis=-1, keepdims=True) + EPS
    bs1[...] = unit_back(item, i_total, item_grad).astype(BF).reshape(bs1.shape)
    br1[z] = bs1[z]
    back_z = exchange(at_z, nz, z, lambda p: bs1.at[p], lambda me: br1.at[me])
    query_grad = SCALE * (wacc[...] / denom + less * positive)
    query_back = unit_back(raw, q_total, query_grad).astype(BF)

    part = term.shape[1] // nc

    def core_send(a):
        if nc == 1:
            return []
        other = pl.multiple_of((1 - core) * part, part)
        sc[a] = term[a, pl.ds(other, part), :].astype(BF)
        return exchange(at_c, nc, core, lambda p: sc.at[a], lambda me: rc.at[a])

    def core_sum(a):
        own = term[a, pl.ds(pl.multiple_of(core * part, part), part), :]
        return own + rc[a].astype(F32) if nc > 1 else own

    px, py = part // nx, part // nx // ny

    def ring_send(value, n, me, at, src, dst, a):
        src[a] = value.astype(BF).reshape(src.shape[1:])
        return exchange(at, n, me, lambda p: src.at[a, p], lambda me: dst.at[a, me])

    def ring_sum(value_ref, recv, n, me, a):
        total = value_ref
        for k in range(1, n):
            total = total + recv[a, lax.rem(me + k, n)].astype(F32)
        return total

    term[0] = dot(qt[...], query_back)
    c_q = core_send(0)
    arrive(back_z)
    order = pick(lax.broadcasted_iota(jnp.int32, square, 0) == slot_of(lax.broadcasted_iota(jnp.int32, square, 1)))
    bs2[...] = dot(order, br1[...].reshape(slots, -1)).astype(BF).reshape(bs2.shape)
    br2[y] = bs2[y]
    back_y = exchange(at_y, ny, y, lambda p: bs2.at[p], lambda me: br2.at[me])

    def x_send(a):
        value = core_sum(a)
        term[a, pl.ds(0, part), :] = value
        return ring_send(value, nx, x, at_x, sx, rx, a)

    def y_send(a):
        own = term[a, pl.ds(pl.multiple_of(x * px, px), px), :]
        value = ring_sum(own, rx, nx, x, a)
        term[a, pl.ds(0, px), :] = value
        return ring_send(value, ny, y, at_y, sy, ry, a)

    def z_value(a):
        own = term[a, pl.ds(pl.multiple_of(y * py, py), py), :]
        return ring_sum(own, ry, ny, y, a)

    arrive(c_q)
    x_q = x_send(0)
    arrive(back_y)
    owned = dot(mt[...], br2[...].reshape(slots, -1))
    term[1] = split_dot(tt[...], owned)
    c_i = core_send(1)
    arrive(x_q)
    y_q = y_send(0)
    arrive(c_i)
    x_i = x_send(1)
    arrive(y_q)
    zs[0] = z_value(0).astype(BF)
    arrive(x_i)
    y_i = y_send(1)
    arrive(y_i)
    zs[1] = z_value(1).astype(BF)
    rz[z] = zs[...]
    arrive(exchange(at_z, nz, z, lambda p: zs, lambda me: rz.at[me]))
    fin[core, x, y] = jnp.sum(rz[...].astype(F32), axis=0).astype(BF)
    mine = lambda me: fin.at[core, x, y]
    arrive(exchange(at_y, ny, y, lambda p: fin.at[core, x, y], mine))
    arrive(exchange(at_x, nx, x, lambda p: fin.at[core, x], lambda me: fin.at[core, x]))
    arrive(exchange(at_c, nc, core, lambda p: fin.at[core], lambda me: fin.at[core]))

    sums = fin[...].astype(F32)
    squares = jnp.sum(jnp.sum(sums * sums, axis=(0, 1, 2, 3)), keepdims=True)
    limit = math.sqrt(2.0 * outq_ref.shape[0] * outq_ref.shape[1])
    factor = jnp.minimum(1.0, limit / jnp.sqrt(squares + EPS))
    outq_ref[...] = (sums[:, :, :, 0].reshape(outq_ref.shape) * factor).astype(BF)
    outi_ref[...] = (sums[:, :, :, 1].reshape(outi_ref.shape) * factor).astype(BF)
    for one in sems.open:
        one.wait_send()


def per_device(sizes, queries, query_weight, item_weight, table, queue, requests, inverse, write_owner):
    nx, ny, nz, nc = sizes
    ns = ny * nz
    slots = ns * CAP
    width, embed = query_weight.shape
    n_q, n_t = queries.shape[0], table.shape[0]
    n_r = queue.shape[0] // 2
    s = lax.axis_index("shard")
    lane = jnp.arange(slots, dtype=jnp.int32)[None, :]
    ids = jnp.where(lane // CAP == s, jnp.tile(jnp.maximum(requests, 0), (1, ns)), 0)
    part = width // nc
    px, py = part // nx, part // nx // ny
    vm = lambda shape, dtype: pltpu.VMEM(shape, dtype)
    zrows, yrows = ny * CAP, nz * CAP
    scratch = [
        vm((2, nz, ny, n_r, embed), BF),
        vm((width, n_q), BF),
        vm((width, n_t), BF),
        vm((n_t, embed), BF),
        vm((n_q, embed), F32),
        vm((n_q, embed), BF),
        vm((n_q, embed), F32),
        vm((n_q, 128), F32),
        vm((n_t, slots), BF),
        vm((slots, n_q), BF),
        vm((slots, embed), F32),
        vm((n_q, embed), F32),
        vm((ny, nz, slots), jnp.int32),
        vm((nz, nz, slots), jnp.int32),
        vm((nz, slots), jnp.int32),
        vm((ny, yrows, embed), BF),
        vm((ny, yrows, embed), BF),
        vm((nz, zrows, embed), BF),
        vm((nz, zrows, embed), BF),
        vm((16, embed), BF),
        vm((ny, 16, embed), BF),
        vm((16, embed), BF),
        vm((nz, 16, embed), BF),
        vm((nz, zrows, embed), BF),
        vm((nz, zrows, embed), BF),
        vm((ny, yrows, embed), BF),
        vm((ny, yrows, embed), BF),
        vm((2, width, embed), F32),
        vm((2, part, embed), BF),
        vm((2, part, embed), BF),
        vm((2, nx, px, embed), BF),
        vm((2, nx, px, embed), BF),
        vm((2, ny, py, embed), BF),
        vm((2, ny, py, embed), BF),
        vm((2, py, embed), BF),
        vm((nz, 2, py, embed), BF),
        vm((nc, nx, ny, 2, py, embed), BF),
        pltpu.SemaphoreType.DMA((n_sems(sizes),)),
        pltpu.SemaphoreType.DMA((n_sems(sizes),)),
    ]
    full = pl.BlockSpec(memory_space=pltpu.VMEM)
    out_q, out_i, fresh = pl.pallas_call(
        functools.partial(kernel, sizes),
        out_shape=[
            jax.ShapeDtypeStruct((width, embed), BF),
            jax.ShapeDtypeStruct((width, embed), BF),
            jax.ShapeDtypeStruct((ns, embed), BF),
        ],
        in_specs=[full] * 7,
        out_specs=[full] * 3,
        scratch_shapes=scratch,
        compiler_params=pltpu.CompilerParams(
            collective_id=0, has_side_effects=True, vmem_limit_bytes=48 * 2**20
        ),
        name="step",
    )(queries, query_weight, item_weight, table, queue, ids, inverse.reshape(1, n_q))
    updated = jnp.concatenate([fresh, queue[ns:]], axis=0)
    new_queue = jnp.where(s == write_owner[0], updated, queue)
    return out_q, out_i, new_queue


def solution(mesh, sizes=(4, 8, 8, 2)):
    placed = (
        P(("dp", "shard"), None),
        P(),
        P(),
        P("shard", None),
        P(("dp", "shard"), None),
        P(("dp", "shard"), None),
        P(("dp", "shard")),
        P(),
    )
    return jax.shard_map(
        functools.partial(per_device, sizes),
        mesh=mesh,
        in_specs=placed,
        out_specs=(P(), P(), P(("dp", "shard"), None)),
        check_vma=False,
    )
```

time: 425 us -> 116 us (0.27)
  waiting for transfers between devices: 297 us -> 0 us
  Pallas kernels: 0 us -> 106 us
  blocking collectives: 64.6 us -> 0 us
  matrix products: 23.9 us -> 0 us
  between operations: 16.2 us -> 1.36 us
  other arithmetic: 6.97 us -> 1.35 us
  starting transfers between devices: 4.71 us -> 0 us
    psum x1 -> x0, waiting for transfers between devices: 243 us -> none  [per_device(): query_sum, item_sum = lax.psum((query_term, item_term), ('dp', 'shard'))]
    pallas_call x0 -> x1, Pallas kernels: none -> 106 us  [per_device(): pl.pallas_call(functools.partial(kernel, sizes), out_shape=[jax.ShapeDtyp...]
    all_gather x1 -> x0, waiting for transfers between devices: 39.5 us -> none  [per_device(): shard_piece = lax.all_gather(queue, 'shard', axis=0, tiled=True)]
    all_gather x1 -> x0, blocking collectives: 36.8 us -> none  [per_device(): all_fresh = lax.all_gather(fresh_embed, 'shard', axis=0, tiled=True)]
    all_to_all x1 -> x0, blocking collectives: 27.8 us -> none  [per_device(): lax.all_to_all(requests, 'shard', split_axis=0, concat_axis=0, tiled=True)]
    dot_general x7 -> x0, matrix products: 23.9 us -> none  [the longest x1 9.7 us: per_device(): jnp.einsum('qe,ne->qn', query_embed, shard_piece, preferred_element_type=...]
    all_to_all x1 -> x0, waiting for transfers between devices: 14.5 us -> none  [per_device(): lax.all_to_all(looked, 'shard', split_axis=0, concat_axis=0, tiled=True)]
    gather x4 -> x0, local copies, waits for them, and re-layouts: 5.75 us -> none  [the longest x2 3.66 us: per_device(): table[jnp.maximum(lax.all_to_all(requests, 'shard', split_axis=0, concat_...]
  transfers between devices with their start and end apart: 3 -> 0, of which waited for: 3 -> 0; matrix products, arithmetic and copies ran while one was open for 3% -> 0% of each run, Pallas kernels for 0% -> 0%
where the time goes in v1:
time: 116 us; the launch traced here: 115 us
  Pallas kernels  106 us (91%)
  local copies, waits for them, and re-layouts  6.94 us (6%)
  between operations  1.36 us (1%)
  other arithmetic  1.35 us (1%)
    pallas_call x1, Pallas kernels, per_device(): pl.pallas_call(functools.partial(kernel, sizes), out_shape=[jax.ShapeDtyp...  106 us
    unnamed x14, local copies, waits for them, and re-layouts  6.75 us

profile of v1, /device:TPU:1, one launch (start us, length us, event | category | flops | bytes accessed | tf_op | source)
XLA Modules:
  0.0 115.4 jit_solution(2534624311277929647)
XLA Ops:
  0.6 0.7 broadcast_maximum_fusion
  1.3 0.1 copy.12
  1.4 0.0 copy-start.4
  1.5 0.0 copy-start.5
  1.5 0.8 copy-done.4
  2.3 0.0 copy-done.5
  2.3 0.0 copy-start
  2.3 1.2 %copy-done = bf16[512,1024]{1,0:T(8,128)(2,1)S(1)} copy-done((bf16[512,1024]{1,0:T(8,128)(2,1)S(1)}, bf16[512,1024]{1,0:T(8,128)(2,1)}, u32[]{:S(2)}) %copy-start) | copy-done | bytes 1048600
  3.5 0.0 copy-start.1
  3.5 1.0 copy-done.1
  4.6 0.0 copy-start.2
  4.6 1.0 copy-done.2
  5.6 0.0 copy-start.3
  5.6 1.0 copy-done.3
  6.6 105.8 %step.1 = (bf16[1024,256]{1,0:T(8,128)(2,1)S(1)}, bf16[1024,256]{1,0:T(8,128)(2,1)S(1)}, bf16[64,256]{1,0:T(8,128)(2,1)S(1)}) custom-call(bf16[512,1024]{1,0:T(8,128)(2,1)S(1)} %copy-done, bf16[1024,256]{1,0:T(8,128)(2,1)S(1)} %copy-done.1, bf16[1024,256]{1,0:T(8,128)(2,1)S(1)} %copy-done.2, bf16[256,1024]{1,0:T(8,128)(2,1)S(1)} %copy-done.3, ...), custom_call_target="tpu_custom_call" | custom-call | tf_op jit(solution)/shard_map/step/pallas_call | solution.py:389
  112.4 0.0 slice-start
  113.1 0.1 slice-done
  113.2 0.6 maximum_select_fusion
  113.8 0.8 copy.16
  114.6 0.8 copy.17
  (3 shorter events, 0.0 us)
Async XLA Ops:
  1.4 0.8 copy-start.4
  1.5 0.8 copy-start.5
  2.3 1.2 %copy-start = (bf16[512,1024]{1,0:T(8,128)(2,1)S(1)}, bf16[512,1024]{1,0:T(8,128)(2,1)}, u32[]{:S(2)}) copy-start(bf16[512,1024]{1,0:T(8,128)(2,1)} %q_ref.1) | copy-start | bytes 3145732
  3.5 1.0 copy-start.1
  4.6 1.0 copy-start.2
  5.6 1.0 copy-start.3
  112.4 0.8 slice-start

commit v2 on v1

v2 whole, which is shorter than its diff:
```python
import functools
import math

import jax
import jax.numpy as jnp
from jax import lax
from jax.experimental import pallas as pl
from jax.experimental.pallas import tpu as pltpu
from jax.sharding import PartitionSpec as P

SCALE = 50.0
EPS = 1e-06
CAP = 4
BF = jnp.bfloat16
F32 = jnp.float32
LOG2E = math.log2(math.e)
MESH = pl.DeviceIdType.MESH


def dot(a, b, lhs=1, rhs=0):
    return lax.dot_general(a, b, (((lhs,), (rhs,)), ((), ())), preferred_element_type=F32)


def split_dot(a, wide):
    high = wide.astype(BF)
    low = (wide - high.astype(F32)).astype(BF)
    return dot(a, high) + dot(a, low)


def pick(mask):
    return jnp.where(mask, 1.0, 0.0).astype(BF)


def unit_back(raw, total, grad):
    inner = jnp.sum(raw * grad, axis=-1, keepdims=True)
    inv = lax.rsqrt(total)
    return grad * inv - raw * (inner * inv / total)


class Link:
    def __init__(self, made):
        self.made, self.started, self.arrived = made, False, False

    def start(self):
        self.started = True
        self.made.start()

    def wait_recv(self):
        self.arrived = True
        self.made.wait_recv()


class Sems:
    def __init__(self, send, recv):
        self.send, self.recv, self.used = send, recv, 0
        self.open = []

    def copy(self, src, dst, device):
        i = self.used
        self.used += 1
        made = Link(pltpu.make_async_remote_copy(
            src_ref=src, dst_ref=dst, send_sem=self.send.at[i], recv_sem=self.recv.at[i],
            device_id=device, device_id_type=MESH,
        ))
        self.open.append(made)
        return made

    def finish(self):
        for one in self.open:
            if one.started and not one.arrived:
                one.wait_recv()
        for one in self.open:
            if one.started:
                one.made.wait_send()


def n_sems(sizes):
    nx, ny, nz, nc = sizes
    y, z, x, c = ny - 1, nz - 1, nx - 1, nc - 1
    gather = 2 * y + 2 * y * (ny // 2 + 1)
    items = 2 * (y + z) * 2 + (y + z)
    reduce = 2 * (c + x + y) + z + y + (ny // 2 + 1) * (x + c * nx)
    return gather + items + reduce


def kernel(sizes, q_hbm, qw_hbm, iw_hbm, t_hbm, r_ref, req_ref, inv_ref, fin, fresh_ref,
           q_ref, qw_ref, iw_ref, t_ref, local_sem, id_ref, buf, qt, tt, traw, qraw, qe, wacc, dacc, mt, ot, iraw, pos, pos_expo,
           id1, id2, id2s, rs1, rr1, rs2, rr2, fs1, fr1, fs2, fr2, bs1, br1, bs2, br2,
           term, sc, rc, sx, rx, sy, ry, zs, rz, send_sem, recv_sem):
    nx, ny, nz, nc = sizes
    ns = ny * nz
    slots = ns * CAP
    d, s = lax.axis_index("dp"), lax.axis_index("shard")
    x, core = lax.div(d, nc), lax.rem(d, nc)
    y, z = lax.div(s, nz), lax.rem(s, nz)
    at_y = lambda p: (d, p * nz + z)
    at_z = lambda p: (d, y * nz + p)
    at_x = lambda p: (p * nc + core, s)
    at_c = lambda p: (x * nc + p, s)
    sems = Sems(send_sem, recv_sem)
    local = [
        pltpu.make_async_copy(src, dst, local_sem.at[i])
        for i, (src, dst) in enumerate(((t_hbm, t_ref), (iw_hbm, iw_ref), (q_hbm, q_ref), (qw_hbm, qw_ref)))
    ]
    for one in local:
        one.start()
    lane = lax.broadcasted_iota(jnp.int32, (CAP, slots), 1)
    spot = lax.broadcasted_iota(jnp.int32, (CAP, slots), 0)
    asks = jnp.maximum(req_ref[...], 0).astype(F32)
    id_ref[...] = dot(asks, jnp.where(lane == s * CAP + spot, 1.0, 0.0), 0, 0).astype(jnp.int32)

    barrier = pltpu.get_barrier_semaphore()
    total = 0
    for at, n, me in ((at_y, ny, y), (at_z, nz, z), (at_x, nx, x), (at_c, nc, core)):
        for k in range(1, n):
            pl.semaphore_signal(barrier, inc=1, device_id=at(lax.rem(me + k, n)), device_id_type=MESH)
            total += 1
    pl.semaphore_wait(barrier, total)

    def exchange(at, n, me, src, dst):
        made = []
        for k in range(1, n):
            p = lax.rem(me + k, n)
            made.append(sems.copy(src(p), dst(me), at(p)))
        for one in made:
            one.start()
        return made

    def arrive(made):
        for one in made:
            one.wait_recv()

    n = ny
    half = r_ref.shape[0] // 2
    far = n // 2
    pieces = [(0, 1)] + [(2 * k - 1, 2) for k in range(1, far)] + [(n - 1, 1)]
    rightward = {0, far} | set(range(1, n // 4))

    def slot(offset):
        return n - 1 if abs(offset) == far else 2 * offset - 1 if offset > 0 else -2 * offset

    first, second = {}, {}
    axes = (((at_y, y), (at_z, z)), ((at_z, z), (at_y, y)))
    for h in (0, 1):
        (at1, me1), (at2, me2) = axes[h]
        for left in (0, 1):
            turn = 1 if left else -1
            hop = n - 1 if left else 1
            to2 = at2(lax.rem(me2 + hop, n))
            for k in range(1, far + 1):
                if k < far or left == h:
                    src, hops = (r_ref.at[pl.ds(h * half, half)], k) if k < 3 else (buf.at[h, 0, slot(turn * 2)], k - 2)
                    to1 = at1(lax.rem(me1 + hops * hop, n))
                    first[h, left, k] = sems.copy(src, buf.at[h, 0, slot(turn * k)], to1)
                for p, (begin, size) in enumerate(pieces):
                    if k < far or (p in rightward) == (left == 0):
                        at = pl.ds(begin, size)
                        second[h, left, k, p] = sems.copy(
                            buf.at[h, slot(turn * (k - 1)), at], buf.at[h, slot(turn * k), at], to2)

    streams = [(h, left) for h in (0, 1) for left in (0, 1)]

    def send_first(*distances):
        for k in distances:
            for h, left in streams:
                if (h, left, k) in first:
                    first[h, left, k].start()

    def have_first(*distances):
        for k in distances:
            for h, left in streams:
                if (h, left, k) in first:
                    first[h, left, k].wait_recv()

    def send_column(*which):
        for p in which:
            for h, left in streams:
                if (h, left, 1, p) in second:
                    second[h, left, 1, p].start()

    def ring(k, *which):
        for p in which:
            for h, left in streams:
                if (h, left, k, p) in second:
                    second[h, left, k, p].wait_recv()
                    if (h, left, k + 1, p) in second:
                        second[h, left, k + 1, p].start()

    attended = set()

    def attend(h, offset):
        if abs(offset) > far or (h, slot(offset)) in attended:
            return
        col = slot(offset)
        attended.add((h, col))
        sub = n // 2

        def body(t, carry):
            rows = buf[h, col, pl.ds(t * sub, sub)]
            keys = rows.reshape(sub * half, rows.shape[2])
            expo = jnp.exp2(dot(qe[...], keys, 1, 1) * (SCALE * LOG2E))
            wacc[...] += dot(expo.astype(BF), keys)
            lanes = dacc.shape[1]
            dacc[...] += sum(expo[:, k : k + lanes] for k in range(0, expo.shape[1], lanes))
            return carry

        lax.fori_loop(0, 2, body, 0)

    def slot_of(i):
        zo, yo, c = i // (ny * CAP), (i // CAP) % ny, i % CAP
        return (yo * nz + zo) * CAP + c

    square = (slots, slots)
    send_first(1, 2)
    ids_y = exchange(at_y, ny, y, lambda p: id_ref.at[pl.ds(pl.multiple_of(p * nz, nz), nz)], lambda me: id1.at[me])
    buf[0, 0, 0] = r_ref[pl.ds(0, half), :]
    buf[1, 0, 0] = r_ref[pl.ds(half, half), :]
    send_column(0)
    id1[y] = id_ref[pl.ds(pl.multiple_of(y * nz, nz), nz), :]
    wacc[...] = jnp.zeros_like(wacc)
    dacc[...] = jnp.zeros_like(dacc)
    local[0].wait()
    local[1].wait()
    traw[...] = dot(t_ref[...], iw_ref[...]).astype(BF)
    have_first(1, 2)
    send_first(3, 4)
    send_column(1, 2)
    ring(1, 0)
    local[2].wait()
    local[3].wait()
    raw = dot(q_ref[...], qw_ref[...])
    qraw[...] = raw
    q_total = jnp.sum(raw * raw, axis=-1, keepdims=True) + EPS
    qe[...] = (raw * lax.rsqrt(q_total)).astype(BF)
    arrive(ids_y)
    id2s[...] = jnp.sum(id1[...], axis=0)
    id2[z] = id2s[...]
    ids_z = exchange(at_z, nz, z, lambda p: id2s, lambda me: id2.at[me])
    have_first(3, 4)
    send_column(3, 4)
    ring(1, 1)
    qt[...] = q_ref[...].T
    ring(1, 2)

    arrive(ids_z)
    mine = lax.broadcasted_iota(jnp.int32, (nz, slots), 0) == z
    asked = jnp.sum(jnp.where(mine, jnp.sum(id2[...], axis=0), 0), axis=0, keepdims=True)
    mt[...] = pick(lax.broadcasted_iota(jnp.int32, mt.shape, 0) == asked)
    rs1[...] = dot(mt[...], traw[...], 0, 0).astype(BF).reshape(rs1.shape)
    rr1[y] = rs1[y]
    rows_y = exchange(at_y, ny, y, lambda p: rs1.at[p], lambda me: rr1.at[me])
    ring(1, 3)
    attend(0, 0)
    ring(1, 4)
    attend(1, 0)
    ring(2, 0)
    attend(0, -1)
    ring(2, 1)
    attend(1, -1)
    ring(2, 2)
    attend(0, 1)
    ring(2, 3)
    attend(1, 1)
    ring(2, 4)
    arrive(rows_y)
    order = pick(lax.broadcasted_iota(jnp.int32, square, 1) == slot_of(lax.broadcasted_iota(jnp.int32, square, 0)))
    rs2[...] = dot(order, rr1[...].reshape(slots, -1)).astype(BF).reshape(rs2.shape)
    rr2[z] = rs2[z]
    rows_z = exchange(at_z, nz, z, lambda p: rs2.at[p], lambda me: rr2.at[me])
    ring(3, 0)
    attend(0, -2)
    ring(3, 1)
    attend(1, -2)
    ring(3, 2)
    attend(0, 2)
    ring(3, 3)
    attend(1, 2)
    ring(3, 4)
    tt[...] = t_ref[...].T

    arrive(rows_z)
    item = rr2[...].reshape(slots, -1).astype(F32)
    iraw[...] = item
    i_total = jnp.sum(item * item, axis=-1, keepdims=True) + EPS
    embed = (item * lax.rsqrt(i_total)).astype(BF)
    slot_rows = slot_of(lax.broadcasted_iota(jnp.int32, ot.shape, 0))
    ot[...] = pick(slot_rows == inv_ref[...])
    pos[...] = dot(ot[...], embed, 0, 0)
    pos_expo[...] = jnp.exp(SCALE * jnp.sum(qe[...].astype(F32) * pos[...], axis=1, keepdims=True))
    head = jnp.broadcast_to(pos[0:1, :], fs1.shape)
    fs1[...] = jnp.where(lax.broadcasted_iota(jnp.int32, fs1.shape, 0) == y, head, 0.0).astype(BF)
    fr1[y] = fs1[...]
    fresh_y = exchange(at_y, ny, y, lambda p: fs1, lambda me: fr1.at[me])
    ring(4, 0)
    attend(0, -3)
    ring(4, 1)
    attend(1, -3)
    ring(4, 2)
    attend(0, 3)
    ring(4, 3)
    attend(1, 3)
    ring(4, 4)
    attend(0, -4)
    attend(1, -4)

    raw = qraw[...]
    q_total = jnp.sum(raw * raw, axis=-1, keepdims=True) + EPS
    embed = qe[...].astype(F32)
    positive = pos[...]
    denom = pos_expo[...] + jnp.sum(dacc[...], axis=1, keepdims=True)
    less = pos_expo[...] / denom - 1.0
    item_grad = split_dot(ot[...], (SCALE * less) * embed)
    item = iraw[...]
    i_total = jnp.sum(item * item, axis=-1, keepdims=True) + EPS
    bs1[...] = unit_back(item, i_total, item_grad).astype(BF).reshape(bs1.shape)
    br1[z] = bs1[z]
    back_z = exchange(at_z, nz, z, lambda p: bs1.at[p], lambda me: br1.at[me])
    query_grad = SCALE * (wacc[...] / denom + less * positive)
    query_back = unit_back(raw, q_total, query_grad).astype(BF)

    part = term.shape[1] // nc

    def core_send(a):
        if nc == 1:
            return []
        other = pl.multiple_of((1 - core) * part, part)
        sc[a] = term[a, pl.ds(other, part), :].astype(BF)
        return exchange(at_c, nc, core, lambda p: sc.at[a], lambda me: rc.at[a])

    def core_sum(a):
        own = term[a, pl.ds(pl.multiple_of(core * part, part), part), :]
        return own + rc[a].astype(F32) if nc > 1 else own

    px, py = part // nx, part // nx // ny

    def ring_send(value, n, me, at, src, dst, a):
        src[a] = value.astype(BF).reshape(src.shape[1:])
        return exchange(at, n, me, lambda p: src.at[a, p], lambda me: dst.at[a, me])

    def ring_sum(value_ref, recv, n, me, a):
        total = value_ref
        for k in range(1, n):
            total = total + recv[a, lax.rem(me + k, n)].astype(F32)
        return total

    arrive(fresh_y)
    fs2[...] = jnp.sum(fr1[...].astype(F32), axis=0).astype(BF)
    fr2[z] = fs2[...]
    fresh_z = exchange(at_z, nz, z, lambda p: fs2, lambda me: fr2.at[me])

    term[0] = dot(qt[...], query_back)
    c_q = core_send(0)
    arrive(back_z)
    order = pick(lax.broadcasted_iota(jnp.int32, square, 0) == slot_of(lax.broadcasted_iota(jnp.int32, square, 1)))
    bs2[...] = dot(order, br1[...].reshape(slots, -1)).astype(BF).reshape(bs2.shape)
    br2[y] = bs2[y]
    back_y = exchange(at_y, ny, y, lambda p: bs2.at[p], lambda me: br2.at[me])

    def x_send(a):
        value = core_sum(a)
        term[a, pl.ds(0, part), :] = value
        return ring_send(value, nx, x, at_x, sx, rx, a)

    def y_send(a):
        own = term[a, pl.ds(pl.multiple_of(x * px, px), px), :]
        value = ring_sum(own, rx, nx, x, a)
        term[a, pl.ds(0, px), :] = value
        return ring_send(value, ny, y, at_y, sy, ry, a)

    def z_value(a):
        own = term[a, pl.ds(pl.multiple_of(y * py, py), py), :]
        return ring_sum(own, ry, ny, y, a)

    arrive(c_q)
    x_q = x_send(0)
    arrive(back_y)
    owned = dot(mt[...], br2[...].reshape(slots, -1))
    term[1] = split_dot(tt[...], owned)
    c_i = core_send(1)
    arrive(x_q)
    y_q = y_send(0)
    arrive(c_i)
    x_i = x_send(1)
    arrive(y_q)
    zs[0] = z_value(0).astype(BF)
    arrive(x_i)
    y_i = y_send(1)
    arrive(y_i)
    zs[1] = z_value(1).astype(BF)
    rz[z] = zs[...]
    arrive(exchange(at_z, nz, z, lambda p: zs, lambda me: rz.at[me]))
    fin[core, x, 0] = jnp.sum(rz[...].astype(F32), axis=0).astype(BF)
    groups = [(p,) + piece for p, piece in enumerate(pieces)]
    along_y = {}
    for k in range(1, ny):
        offset = ny - k if ny - k <= far else -k
        along_y[k] = sems.copy(fin.at[core, x, 0], fin.at[core, x, slot(offset)], at_y(lax.rem(y + k, ny)))
        along_y[k].start()

    to_core = []

    def hand_over(xx, begin, size):
        if nc > 1:
            ref = fin.at[core, xx, pl.ds(begin, size)]
            to_core.append(sems.copy(ref, ref, at_c(1 - core)))
            to_core[-1].start()

    along_x = {}
    for p, begin, size in groups:
        for k in sorted({p, ny - p}) if p else ():
            along_y[k].wait_recv()
        ref = fin.at[core, x, pl.ds(begin, size)]
        for k in range(1, nx):
            along_x[p, k] = sems.copy(ref, ref, at_x(lax.rem(x + k, nx)))
            along_x[p, k].start()
        hand_over(x, begin, size)
    arrive(fresh_z)
    fshape = (ns, nz * fs2.shape[0])
    want = lax.broadcasted_iota(jnp.int32, fshape, 0)
    place = (want % nz) * fs2.shape[0] + want // nz
    fresh_ref[...] = dot(pick(lax.broadcasted_iota(jnp.int32, fshape, 1) == place),
                         fr2[...].reshape(fshape[1], -1)).astype(BF)
    for p, begin, size in groups:
        for k in range(1, nx):
            along_x[p, k].wait_recv()
            hand_over(lax.rem(x + nx - k, nx), begin, size)
    arrive(to_core)

    sems.finish()


def clip(nz, sums_ref, fresh_ref, queue_ref, owner_ref, outq, outi, outn, sq, si, sn, sem):
    s = lax.axis_index("shard")
    ny = sums_ref.shape[2]
    y = lax.div(s, nz)
    ns = fresh_ref.shape[0]
    mine = owner_ref[0] == s
    sn[pl.ds(0, ns), :] = jnp.where(mine, fresh_ref[...], queue_ref[pl.ds(0, ns), :])
    sn[pl.ds(ns, sn.shape[0] - ns), :] = queue_ref[pl.ds(ns, sn.shape[0] - ns), :]
    made = [pltpu.make_async_copy(src, dst, sem.at[i]) for i, (src, dst) in enumerate(((sn, outn), (sq, outq), (si, outi)))]
    made[0].start()
    sums = sums_ref[...].astype(F32)
    squares = jnp.sum(jnp.sum(sums * sums, axis=(0, 1, 2, 3)), keepdims=True)
    count = math.prod(sums_ref.shape)
    factor = jnp.minimum(1.0, math.sqrt(count) / jnp.sqrt(squares + EPS))
    for a, out in enumerate((sq, si)):
        for row in range(ny):
            ahead = lax.rem(row - y + ny, ny)
            at = jnp.where(ahead == 0, 0, jnp.where(ahead < ny // 2, 2 * ahead - 1, 2 * (ny - ahead)))
            at = jnp.where(ahead == ny // 2, ny - 1, at)
            out[:, :, row] = (sums_ref[:, :, at, a].astype(F32) * factor).astype(BF)
        made[1 + a].start()
    for one in made:
        one.wait()


def per_device(sizes, queries, query_weight, item_weight, table, queue, requests, inverse, write_owner):
    nx, ny, nz, nc = sizes
    ns = ny * nz
    slots = ns * CAP
    width, embed = query_weight.shape
    n_q, n_t = queries.shape[0], table.shape[0]
    n_r = queue.shape[0] // 2
    s = lax.axis_index("shard")
    part = width // nc
    px, py = part // nx, part // nx // ny
    vm = lambda shape, dtype: pltpu.VMEM(shape, dtype)
    zrows, yrows = ny * CAP, nz * CAP
    scratch = [
        vm(queries.shape, BF),
        vm(query_weight.shape, BF),
        vm(item_weight.shape, BF),
        vm(table.shape, BF),
        pltpu.SemaphoreType.DMA((4,)),
        vm((ns, slots), jnp.int32),
        vm((2, nz, ny, n_r, embed), BF),
        vm((width, n_q), BF),
        vm((width, n_t), BF),
        vm((n_t, embed), BF),
        vm((n_q, embed), F32),
        vm((n_q, embed), BF),
        vm((n_q, embed), F32),
        vm((n_q, 128), F32),
        vm((n_t, slots), BF),
        vm((slots, n_q), BF),
        vm((slots, embed), F32),
        vm((n_q, embed), F32),
        vm((n_q, 1), F32),
        vm((ny, nz, slots), jnp.int32),
        vm((nz, nz, slots), jnp.int32),
        vm((nz, slots), jnp.int32),
        vm((ny, yrows, embed), BF),
        vm((ny, yrows, embed), BF),
        vm((nz, zrows, embed), BF),
        vm((nz, zrows, embed), BF),
        vm((16, embed), BF),
        vm((ny, 16, embed), BF),
        vm((16, embed), BF),
        vm((nz, 16, embed), BF),
        vm((nz, zrows, embed), BF),
        vm((nz, zrows, embed), BF),
        vm((ny, yrows, embed), BF),
        vm((ny, yrows, embed), BF),
        vm((2, width, embed), F32),
        vm((2, part, embed), BF),
        vm((2, part, embed), BF),
        vm((2, nx, px, embed), BF),
        vm((2, nx, px, embed), BF),
        vm((2, ny, py, embed), BF),
        vm((2, ny, py, embed), BF),
        vm((2, py, embed), BF),
        vm((nz, 2, py, embed), BF),
        pltpu.SemaphoreType.DMA((n_sems(sizes),)),
        pltpu.SemaphoreType.DMA((n_sems(sizes),)),
    ]
    full = pl.BlockSpec(memory_space=pltpu.VMEM)
    far = pl.BlockSpec(memory_space=pl.ANY)
    sums, fresh = pl.pallas_call(
        functools.partial(kernel, sizes),
        out_shape=[
            jax.ShapeDtypeStruct((nc, nx, ny, 2, py, embed), BF),
            jax.ShapeDtypeStruct((ns, embed), BF),
        ],
        in_specs=[far] * 4 + [full] * 3,
        out_specs=[full] * 2,
        scratch_shapes=scratch,
        compiler_params=pltpu.CompilerParams(
            collective_id=0, has_side_effects=True, vmem_limit_bytes=56 * 2**20
        ),
        name="step",
    )(queries, query_weight, item_weight, table, queue, requests.T, inverse.reshape(1, n_q))
    laid = (nc, nx, ny, py, embed)
    out_q, out_i, new_queue = pl.pallas_call(
        functools.partial(clip, nz),
        out_shape=[
            jax.ShapeDtypeStruct(laid, BF),
            jax.ShapeDtypeStruct(laid, BF),
            jax.ShapeDtypeStruct(queue.shape, BF),
        ],
        in_specs=[full] * 3 + [pl.BlockSpec(memory_space=pltpu.SMEM)],
        out_specs=[far] * 3,
        scratch_shapes=[
            vm(laid, BF),
            vm(laid, BF),
            vm(queue.shape, BF),
            pltpu.SemaphoreType.DMA((3,)),
        ],
        name="clip",
    )(sums, fresh, queue, write_owner)
    return out_q.reshape(width, embed), out_i.reshape(width, embed), new_queue


def solution(mesh, sizes=(4, 8, 8, 2)):
    placed = (
        P(("dp", "shard"), None),
        P(),
        P(),
        P("shard", None),
        P(("dp", "shard"), None),
        P(("dp", "shard"), None),
        P(("dp", "shard")),
        P(),
    )
    return jax.shard_map(
        functools.partial(per_device, sizes),
        mesh=mesh,
        in_specs=placed,
        out_specs=(P(), P(), P(("dp", "shard"), None)),
        check_vma=False,
    )
```

time: 116 us -> 103 us (0.89)
  local copies, waits for them, and re-layouts: 6.94 us -> 0 us
  Pallas kernels: 106 us -> 102 us
  other arithmetic: 1.35 us -> 0 us
    unnamed x14 -> x0, local copies, waits for them, and re-layouts: 6.75 us -> none
    pallas_call x1, Pallas kernels: 106 us -> 99 us  [per_device(): pl.pallas_call(functools.partial(kernel, sizes), out_shape=[jax.ShapeDtyp...]
    pallas_call x0 -> x1, Pallas kernels: none -> 2.53 us  [per_device(): pl.pallas_call(functools.partial(clip, nz), out_shape=[jax.ShapeDtypeStru...]
where the time goes in v2:
time: 103 us
  Pallas kernels  102 us (99%)
  between operations  1.29 us (1%)
    pallas_call x1, Pallas kernels, per_device(): pl.pallas_call(functools.partial(kernel, sizes), out_shape=[jax.ShapeDtyp...  99 us
    pallas_call x1, Pallas kernels, per_device(): pl.pallas_call(functools.partial(clip, nz), out_shape=[jax.ShapeDtypeStru...  2.53 us

profile of v2, /device:TPU:1, one launch (start us, length us, event | category | flops | bytes accessed | tf_op | source)
XLA Modules:
  0.0 102.9 jit_solution(14766409692919547618)
XLA Ops:
  1.3 99.0 %step.1 = (bf16[2,4,8,2,16,256]{5,4,3,2,1,0:T(8,128)(2,1)}, bf16[64,256]{1,0:T(8,128)(2,1)}) custom-call(bf16[512,1024]{1,0:T(8,128)(2,1)} %q_hbm.1, bf16[1024,256]{1,0:T(8,128)(2,1)} %qw_hbm.1, bf16[1024,256]{1,0:T(8,128)(2,1)} %iw_hbm.1, bf16[256,1024]{1,0:T(8,128)(2,1)} %t_hbm.1, bf16[128,256]{1,0:T(8,128)(2,1)} %queue_ref.1, s32[4,64]{1,0:T(4,128)} %bitcast.4, ...), custom_call_target="tpu_custom_call" | custom-call | tf_op jit(solution)/shard_map/step/pallas_call | solution.py:518
  100.3 2.5 %clip.1 = (bf16[2,4,8,16,256]{4,3,2,1,0:T(8,128)(2,1)}, bf16[2,4,8,16,256]{4,3,2,1,0:T(8,128)(2,1)}, bf16[128,256]{1,0:T(8,128)(2,1)}) custom-call(bf16[2,4,8,2,16,256]{5,4,3,2,1,0:T(8,128)(2,1)} %get-tuple-element.8.sums_ref, bf16[64,256]{1,0:T(8,128)(2,1)} %get-tuple-element.9.fresh_ref, bf16[128,256]{1,0:T(8,128)(2,1)} %queue_ref.1, s32[1]{0:T(128)S(6)} %copy.11.owner_ref), custom_call_target="tpu_custom_call" | custom-call | tf_op jit(solution)/shard_map/clip/pallas_call | solution.py:533

commit v3 on v2

--- a/solution.py
+++ b/solution.py
@@ -79,14 +79,15 @@
     y, z, x, c = ny - 1, nz - 1, nx - 1, nc - 1
     gather = 2 * y + 2 * y * (ny // 2 + 1)
     items = 2 * (y + z) * 2 + (y + z)
-    reduce = 2 * (c + x + y) + z + y + (ny // 2 + 1) * (x + c * nx)
+    groups = ny // 2 + 1
+    reduce = 2 * (c + groups * x + y + z + y + groups * (x + c * nx))
     return gather + items + reduce
 
 
 def kernel(sizes, q_hbm, qw_hbm, iw_hbm, t_hbm, r_ref, req_ref, inv_ref, fin, fresh_ref,
            q_ref, qw_ref, iw_ref, t_ref, local_sem, id_ref, buf, qt, tt, traw, qraw, qe, wacc, dacc, mt, ot, iraw, pos, pos_expo,
            id1, id2, id2s, rs1, rr1, rs2, rr2, fs1, fr1, fs2, fr2, bs1, br1, bs2, br2,
-           term, sc, rc, sx, rx, sy, ry, zs, rz, send_sem, recv_sem):
+           term, sc, rc, sx, rx, sy, ry, mine_f32, zs, rz, send_sem, recv_sem):
     nx, ny, nz, nc = sizes
     ns = ny * nz
     slots = ns * CAP
@@ -100,7 +101,11 @@
     sems = Sems(send_sem, recv_sem)
     local = [
         pltpu.make_async_copy(src, dst, local_sem.at[i])
-        for i, (src, dst) in enumerate(((t_hbm, t_ref), (iw_hbm, iw_ref), (q_hbm, q_ref), (qw_hbm, qw_ref)))
+        for i, (src, dst) in enumerate((
+            (t_hbm, t_ref), (iw_hbm, iw_ref), (q_hbm, q_ref), (qw_hbm, qw_ref),
+            (r_ref.at[pl.ds(0, r_ref.shape[0] // 2)], buf.at[0, 0, 0]),
+            (r_ref.at[pl.ds(r_ref.shape[0] // 2, r_ref.shape[0] // 2)], buf.at[1, 0, 0]),
+        ))
     ]
     for one in local:
         one.start()
@@ -155,8 +160,10 @@
                 for p, (begin, size) in enumerate(pieces):
                     if k < far or (p in rightward) == (left == 0):
                         at = pl.ds(begin, size)
-                        second[h, left, k, p] = sems.copy(
-                            buf.at[h, slot(turn * (k - 1)), at], buf.at[h, slot(turn * k), at], to2)
+                        src, dst = buf.at[h, slot(turn * (k - 1)), at], buf.at[h, slot(turn * k), at]
+                        if k == 1 and p == 0:
+                            src, dst = r_ref.at[pl.ds(h * half, half)], buf.at[h, slot(turn), 0]
+                        second[h, left, k, p] = sems.copy(src, dst, to2)
 
     streams = [(h, left) for h in (0, 1) for left in (0, 1)]
 
@@ -188,23 +195,20 @@
 
     attended = set()
 
-    def attend(h, offset):
-        if abs(offset) > far or (h, slot(offset)) in attended:
-            return
-        col = slot(offset)
-        attended.add((h, col))
-        sub = n // 2
-
-        def body(t, carry):
-            rows = buf[h, col, pl.ds(t * sub, sub)]
-            keys = rows.reshape(sub * half, rows.shape[2])
-            expo = jnp.exp2(dot(qe[...], keys, 1, 1) * (SCALE * LOG2E))
-            wacc[...] += dot(expo.astype(BF), keys)
+    def attend(*which):
+        parts = []
+        for h in (0, 1):
+            for offset in which:
+                if abs(offset) > far or (h, slot(offset)) in attended:
+                    continue
+                attended.add((h, slot(offset)))
+                rows = buf[h, slot(offset)]
+                keys = rows.reshape(n * half, rows.shape[2])
+                parts.append((keys, jnp.exp2(dot(qe[...], keys, 1, 1) * (SCALE * LOG2E))))
+        if parts:
+            wacc[...] += sum(dot(expo.astype(BF), keys) for keys, expo in parts)
             lanes = dacc.shape[1]
-            dacc[...] += sum(expo[:, k : k + lanes] for k in range(0, expo.shape[1], lanes))
-            return carry
-
-        lax.fori_loop(0, 2, body, 0)
+            dacc[...] += sum(expo[:, k : k + lanes] for _, expo in parts for k in range(0, expo.shape[1], lanes))
 
     def slot_of(i):
         zo, yo, c = i // (ny * CAP), (i // CAP) % ny, i % CAP
@@ -213,8 +217,6 @@
     square = (slots, slots)
     send_first(1, 2)
     ids_y = exchange(at_y, ny, y, lambda p: id_ref.at[pl.ds(pl.multiple_of(p * nz, nz), nz)], lambda me: id1.at[me])
-    buf[0, 0, 0] = r_ref[pl.ds(0, half), :]
-    buf[1, 0, 0] = r_ref[pl.ds(half, half), :]
     send_column(0)
     id1[y] = id_ref[pl.ds(pl.multiple_of(y * nz, nz), nz), :]
     wacc[...] = jnp.zeros_like(wacc)
@@ -226,8 +228,8 @@
     send_first(3, 4)
     send_column(1, 2)
     ring(1, 0)
-    local[2].wait()
-    local[3].wait()
+    for one in local[2:]:
+        one.wait()
     raw = dot(q_ref[...], qw_ref[...])
     qraw[...] = raw
     q_total = jnp.sum(raw * raw, axis=-1, keepdims=True) + EPS
@@ -250,34 +252,27 @@
     rr1[y] = rs1[y]
     rows_y = exchange(at_y, ny, y, lambda p: rs1.at[p], lambda me: rr1.at[me])
     ring(1, 3)
-    attend(0, 0)
+    attend(0)
     ring(1, 4)
-    attend(1, 0)
-    ring(2, 0)
-    attend(0, -1)
-    ring(2, 1)
-    attend(1, -1)
-    ring(2, 2)
-    attend(0, 1)
-    ring(2, 3)
-    attend(1, 1)
+    ring(2, 0, 1)
+    attend(-1)
+    ring(2, 2, 3)
+    attend(1)
     ring(2, 4)
     arrive(rows_y)
     order = pick(lax.broadcasted_iota(jnp.int32, square, 1) == slot_of(lax.broadcasted_iota(jnp.int32, square, 0)))
     rs2[...] = dot(order, rr1[...].reshape(slots, -1)).astype(BF).reshape(rs2.shape)
     rr2[z] = rs2[z]
     rows_z = exchange(at_z, nz, z, lambda p: rs2.at[p], lambda me: rr2.at[me])
-    ring(3, 0)
-    attend(0, -2)
-    ring(3, 1)
-    attend(1, -2)
-    ring(3, 2)
-    attend(0, 2)
-    ring(3, 3)
-    attend(1, 2)
+    ring(3, 0, 1)
+    attend(-2)
+    ring(3, 2, 3)
+    attend(2)
     ring(3, 4)
     tt[...] = t_ref[...].T
 
+    attend(-3, 3)
+    ring(4, 0, 1)
     arrive(rows_z)
     item = rr2[...].reshape(slots, -1).astype(F32)
     iraw[...] = item
@@ -291,17 +286,8 @@
     fs1[...] = jnp.where(lax.broadcasted_iota(jnp.int32, fs1.shape, 0) == y, head, 0.0).astype(BF)
     fr1[y] = fs1[...]
     fresh_y = exchange(at_y, ny, y, lambda p: fs1, lambda me: fr1.at[me])
-    ring(4, 0)
-    attend(0, -3)
-    ring(4, 1)
-    attend(1, -3)
-    ring(4, 2)
-    attend(0, 3)
-    ring(4, 3)
-    attend(1, 3)
-    ring(4, 4)
-    attend(0, -4)
-    attend(1, -4)
+    ring(4, 2, 3, 4)
+    attend(-4)
 
     raw = qraw[...]
     q_total = jnp.sum(raw * raw, axis=-1, keepdims=True) + EPS
@@ -332,16 +318,87 @@
         return own + rc[a].astype(F32) if nc > 1 else own
 
     px, py = part // nx, part // nx // ny
-
-    def ring_send(value, n, me, at, src, dst, a):
-        src[a] = value.astype(BF).reshape(src.shape[1:])
-        return exchange(at, n, me, lambda p: src.at[a, p], lambda me: dst.at[a, me])
-
-    def ring_sum(value_ref, recv, n, me, a):
-        total = value_ref
-        for k in range(1, n):
-            total = total + recv[a, lax.rem(me + k, n)].astype(F32)
-        return total
+    offsets = [0] + [turn * k for k in range(1, far) for turn in (1, -1)] + [far]
+    groups = [(p,) + piece for p, piece in enumerate(pieces)]
+    across = {}
+    along = {}
+
+    def x_send(a):
+        term[a, pl.ds(0, part), :] = core_sum(a)
+        for j, offset in enumerate(offsets):
+            yy = lax.rem(y + offset + ny, ny)
+            for xx in range(nx):
+                rows = pl.ds(pl.multiple_of(xx * px + yy * py, py), py)
+                sx[a, xx, j] = term[a, rows, :].astype(BF)
+        for p, begin, size in groups[::-1]:
+            for k in range(1, nx):
+                to = lax.rem(x + k, nx)
+                at = pl.ds(begin, size)
+                across[a, p, k] = sems.copy(sx.at[a, to, at], rx.at[a, x, at], at_x(to))
+                across[a, p, k].start()
+
+    def y_send(a):
+        for p, begin, size in groups[::-1]:
+            for k in range(1, nx):
+                across[a, p, k].wait_recv()
+            for j in range(begin, begin + size):
+                yy = lax.rem(y + offsets[j] + ny, ny)
+                value = term[a, pl.ds(pl.multiple_of(x * px + yy * py, py), py), :]
+                for k in range(1, nx):
+                    value = value + rx[a, lax.rem(x + k, nx), j].astype(F32)
+                if j == 0:
+                    mine_f32[a] = value
+                else:
+                    sy[a, j] = value.astype(BF)
+                    back = slot(-offsets[j]) if j < ny - 1 else ny - 1
+                    along[a, j] = sems.copy(sy.at[a, j], ry.at[a, back], at_y(yy))
+                    along[a, j].start()
+
+    def z_send(a):
+        value = mine_f32[a]
+        for j in range(1, ny):
+            along[a, j].wait_recv()
+        for j in range(1, ny):
+            value = value + ry[a, j].astype(F32)
+        zs[a] = value.astype(BF)
+        rz[a, z] = zs[a]
+        return exchange(at_z, nz, z, lambda p: zs.at[a], lambda me: rz.at[a, me])
+
+    out_y, out_x, to_core = {}, {}, {0: [], 1: []}
+
+    def hand_over(a, xx, begin, size):
+        if nc > 1:
+            ref = fin.at[a, core, xx, pl.ds(begin, size)]
+            to_core[a].append(sems.copy(ref, ref, at_c(1 - core)))
+            to_core[a][-1].start()
+
+    def out_send(a, p, begin, size):
+        ref = fin.at[a, core, x, pl.ds(begin, size)]
+        for k in range(1, nx):
+            out_x[a, p, k] = sems.copy(ref, ref, at_x(lax.rem(x + k, nx)))
+            out_x[a, p, k].start()
+        hand_over(a, x, begin, size)
+
+    def gather_send(a, arrived):
+        arrive(arrived)
+        fin[a, core, x, 0] = jnp.sum(rz[a].astype(F32), axis=0).astype(BF)
+        for k in range(1, ny):
+            offset = ny - k if ny - k <= far else -k
+            out_y[a, k] = sems.copy(fin.at[a, core, x, 0], fin.at[a, core, x, slot(offset)], at_y(lax.rem(y + k, ny)))
+            out_y[a, k].start()
+        out_send(a, *groups[0])
+
+    def gather_x(a):
+        for p, begin, size in groups[1:]:
+            for k in sorted({p, ny - p}):
+                out_y[a, k].wait_recv()
+            out_send(a, p, begin, size)
+
+    def gather_core(a):
+        for p, begin, size in groups:
+            for k in range(1, nx):
+                out_x[a, p, k].wait_recv()
+                hand_over(a, lax.rem(x + nx - k, nx), begin, size)
 
     arrive(fresh_y)
     fs2[...] = jnp.sum(fr1[...].astype(F32), axis=0).astype(BF)
@@ -350,88 +407,43 @@
 
     term[0] = dot(qt[...], query_back)
     c_q = core_send(0)
+    arrive(c_q)
+    x_send(0)
     arrive(back_z)
     order = pick(lax.broadcasted_iota(jnp.int32, square, 0) == slot_of(lax.broadcasted_iota(jnp.int32, square, 1)))
     bs2[...] = dot(order, br1[...].reshape(slots, -1)).astype(BF).reshape(bs2.shape)
     br2[y] = bs2[y]
     back_y = exchange(at_y, ny, y, lambda p: bs2.at[p], lambda me: br2.at[me])
-
-    def x_send(a):
-        value = core_sum(a)
-        term[a, pl.ds(0, part), :] = value
-        return ring_send(value, nx, x, at_x, sx, rx, a)
-
-    def y_send(a):
-        own = term[a, pl.ds(pl.multiple_of(x * px, px), px), :]
-        value = ring_sum(own, rx, nx, x, a)
-        term[a, pl.ds(0, px), :] = value
-        return ring_send(value, ny, y, at_y, sy, ry, a)
-
-    def z_value(a):
-        own = term[a, pl.ds(pl.multiple_of(y * py, py), py), :]
-        return ring_sum(own, ry, ny, y, a)
-
-    arrive(c_q)
-    x_q = x_send(0)
+    y_send(0)
     arrive(back_y)
     owned = dot(mt[...], br2[...].reshape(slots, -1))
     term[1] = split_dot(tt[...], owned)
     c_i = core_send(1)
-    arrive(x_q)
-    y_q = y_send(0)
+    z_q = z_send(0)
     arrive(c_i)
-    x_i = x_send(1)
-    arrive(y_q)
-    zs[0] = z_value(0).astype(BF)
-    arrive(x_i)
-    y_i = y_send(1)
-    arrive(y_i)
-    zs[1] = z_value(1).astype(BF)
-    rz[z] = zs[...]
-    arrive(exchange(at_z, nz, z, lambda p: zs, lambda me: rz.at[me]))
-    fin[core, x, 0] = jnp.sum(rz[...].astype(F32), axis=0).astype(BF)
-    groups = [(p,) + piece for p, piece in enumerate(pieces)]
-    along_y = {}
-    for k in range(1, ny):
-        offset = ny - k if ny - k <= far else -k
-        along_y[k] = sems.copy(fin.at[core, x, 0], fin.at[core, x, slot(offset)], at_y(lax.rem(y + k, ny)))
-        along_y[k].start()
-
-    to_core = []
-
-    def hand_over(xx, begin, size):
-        if nc > 1:
-            ref = fin.at[core, xx, pl.ds(begin, size)]
-            to_core.append(sems.copy(ref, ref, at_c(1 - core)))
-            to_core[-1].start()
-
-    along_x = {}
-    for p, begin, size in groups:
-        for k in sorted({p, ny - p}) if p else ():
-            along_y[k].wait_recv()
-        ref = fin.at[core, x, pl.ds(begin, size)]
-        for k in range(1, nx):
-            along_x[p, k] = sems.copy(ref, ref, at_x(lax.rem(x + k, nx)))
-            along_x[p, k].start()
-        hand_over(x, begin, size)
+    x_send(1)
+    gather_send(0, z_q)
+    y_send(1)
+    gather_x(0)
+    z_i = z_send(1)
+    gather_core(0)
     arrive(fresh_z)
     fshape = (ns, nz * fs2.shape[0])
     want = lax.broadcasted_iota(jnp.int32, fshape, 0)
     place = (want % nz) * fs2.shape[0] + want // nz
     fresh_ref[...] = dot(pick(lax.broadcasted_iota(jnp.int32, fshape, 1) == place),
                          fr2[...].reshape(fshape[1], -1)).astype(BF)
-    for p, begin, size in groups:
-        for k in range(1, nx):
-            along_x[p, k].wait_recv()
-            hand_over(lax.rem(x + nx - k, nx), begin, size)
-    arrive(to_core)
-
+    arrive(to_core[0])
+    gather_send(1, z_i)
+    gather_x(1)
+    gather_core(1)
+    arrive(to_core[1])
     sems.finish()
 
 
 def clip(nz, sums_ref, fresh_ref, queue_ref, owner_ref, outq, outi, outn, sq, si, sn, sem):
     s = lax.axis_index("shard")
-    ny = sums_ref.shape[2]
+    ny = sums_ref.shape[3]
     y = lax.div(s, nz)
     ns = fresh_ref.shape[0]
     mine = owner_ref[0] == s
@@ -448,7 +460,7 @@
             ahead = lax.rem(row - y + ny, ny)
             at = jnp.where(ahead == 0, 0, jnp.where(ahead < ny // 2, 2 * ahead - 1, 2 * (ny - ahead)))
             at = jnp.where(ahead == ny // 2, ny - 1, at)
-            out[:, :, row] = (sums_ref[:, :, at, a].astype(F32) * factor).astype(BF)
+            out[:, :, row] = (sums_ref[a, :, :, at].astype(F32) * factor).astype(BF)
         made[1 + a].start()
     for one in made:
         one.wait()
@@ -471,7 +483,7 @@
         vm(query_weight.shape, BF),
         vm(item_weight.shape, BF),
         vm(table.shape, BF),
-        pltpu.SemaphoreType.DMA((4,)),
+        pltpu.SemaphoreType.DMA((6,)),
         vm((ns, slots), jnp.int32),
         vm((2, nz, ny, n_r, embed), BF),
         vm((width, n_q), BF),
@@ -504,12 +516,13 @@
         vm((2, width, embed), F32),
         vm((2, part, embed), BF),
         vm((2, part, embed), BF),
-        vm((2, nx, px, embed), BF),
-        vm((2, nx, px, embed), BF),
+        vm((2, nx, ny, py, embed), BF),
+        vm((2, nx, ny, py, embed), BF),
         vm((2, ny, py, embed), BF),
         vm((2, ny, py, embed), BF),
+        vm((2, py, embed), F32),
         vm((2, py, embed), BF),
-        vm((nz, 2, py, embed), BF),
+        vm((2, nz, py, embed), BF),
         pltpu.SemaphoreType.DMA((n_sems(sizes),)),
         pltpu.SemaphoreType.DMA((n_sems(sizes),)),
     ]
@@ -518,10 +531,10 @@
     sums, fresh = pl.pallas_call(
         functools.partial(kernel, sizes),
         out_shape=[
-            jax.ShapeDtypeStruct((nc, nx, ny, 2, py, embed), BF),
+            jax.ShapeDtypeStruct((2, nc, nx, ny, py, embed), BF),
             jax.ShapeDtypeStruct((ns, embed), BF),
         ],
-        in_specs=[far] * 4 + [full] * 3,
+        in_specs=[far] * 5 + [full] * 2,
         out_specs=[full] * 2,
         scratch_shapes=scratch,
         compiler_params=pltpu.CompilerParams(

time: 103 us -> 99.1 us (0.962)
  Pallas kernels: 102 us -> 97.6 us
    pallas_call x1, Pallas kernels: 99 us -> 95.1 us  [per_device(): pl.pallas_call(functools.partial(kernel, sizes), out_shape=[jax.ShapeDtyp...]
where the time goes in v3:
time: 99.1 us; the launch traced here: 98.9 us
  Pallas kernels  97.6 us (98%)
  between operations  1.29 us (1%)
    pallas_call x1, Pallas kernels, per_device(): pl.pallas_call(functools.partial(kernel, sizes), out_shape=[jax.ShapeDtyp...  95.1 us
    pallas_call x1, Pallas kernels, per_device(): pl.pallas_call(functools.partial(clip, nz), out_shape=[jax.ShapeDtypeStru...  2.53 us

profile of v3, /device:TPU:1, one launch (start us, length us, event | category | flops | bytes accessed | tf_op | source)
XLA Modules:
  0.0 98.9 jit_solution(6347794565031325686)
XLA Ops:
  1.3 95.1 %step.1 = (bf16[2,2,4,8,16,256]{5,4,3,2,1,0:T(8,128)(2,1)}, bf16[64,256]{1,0:T(8,128)(2,1)}) custom-call(bf16[512,1024]{1,0:T(8,128)(2,1)} %q_hbm.1, bf16[1024,256]{1,0:T(8,128)(2,1)} %qw_hbm.1, bf16[1024,256]{1,0:T(8,128)(2,1)} %iw_hbm.1, bf16[256,1024]{1,0:T(8,128)(2,1)} %t_hbm.1, bf16[128,256]{1,0:T(8,128)(2,1)} %queue_ref.1, s32[4,64]{1,0:T(4,128)} %bitcast.4, ...), custom_call_target="tpu_custom_call" | custom-call | tf_op jit(solution)/shard_map/step/pallas_call | solution.py:531
  96.4 2.5 %clip.1 = (bf16[2,4,8,16,256]{4,3,2,1,0:T(8,128)(2,1)}, bf16[2,4,8,16,256]{4,3,2,1,0:T(8,128)(2,1)}, bf16[128,256]{1,0:T(8,128)(2,1)}) custom-call(bf16[2,2,4,8,16,256]{5,4,3,2,1,0:T(8,128)(2,1)} %get-tuple-element.8.sums_ref, bf16[64,256]{1,0:T(8,128)(2,1)} %get-tuple-element.9.fresh_ref, bf16[128,256]{1,0:T(8,128)(2,1)} %queue_ref.1, s32[1]{0:T(128)S(6)} %copy.11.owner_ref), custom_call_target="tpu_custom_call" | custom-call | tf_op jit(solution)/shard_map/clip/pallas_call | solution.py:546

commit v4 on v3

--- a/solution.py
+++ b/solution.py
@@ -39,7 +39,7 @@
 
 class Link:
     def __init__(self, made):
-        self.made, self.started, self.arrived = made, False, False
+        self.made, self.started, self.arrived, self.sent = made, False, False, False
 
     def start(self):
         self.started = True
@@ -65,12 +65,18 @@
         self.open.append(made)
         return made
 
+    def drain(self):
+        for one in self.open:
+            if one.started and one.arrived and not one.sent:
+                one.sent = True
+                one.made.wait_send()
+
     def finish(self):
         for one in self.open:
             if one.started and not one.arrived:
                 one.wait_recv()
         for one in self.open:
-            if one.started:
+            if one.started and not one.sent:
                 one.made.wait_send()
 
 
@@ -241,7 +247,6 @@
     have_first(3, 4)
     send_column(3, 4)
     ring(1, 1)
-    qt[...] = q_ref[...].T
     ring(1, 2)
 
     arrive(ids_z)
@@ -269,7 +274,6 @@
     ring(3, 2, 3)
     attend(2)
     ring(3, 4)
-    tt[...] = t_ref[...].T
 
     attend(-3, 3)
     ring(4, 0, 1)
@@ -282,10 +286,6 @@
     ot[...] = pick(slot_rows == inv_ref[...])
     pos[...] = dot(ot[...], embed, 0, 0)
     pos_expo[...] = jnp.exp(SCALE * jnp.sum(qe[...].astype(F32) * pos[...], axis=1, keepdims=True))
-    head = jnp.broadcast_to(pos[0:1, :], fs1.shape)
-    fs1[...] = jnp.where(lax.broadcasted_iota(jnp.int32, fs1.shape, 0) == y, head, 0.0).astype(BF)
-    fr1[y] = fs1[...]
-    fresh_y = exchange(at_y, ny, y, lambda p: fs1, lambda me: fr1.at[me])
     ring(4, 2, 3, 4)
     attend(-4)
 
@@ -301,6 +301,11 @@
     bs1[...] = unit_back(item, i_total, item_grad).astype(BF).reshape(bs1.shape)
     br1[z] = bs1[z]
     back_z = exchange(at_z, nz, z, lambda p: bs1.at[p], lambda me: br1.at[me])
+    head = jnp.broadcast_to(pos[0:1, :], fs1.shape)
+    fs1[...] = jnp.where(lax.broadcasted_iota(jnp.int32, fs1.shape, 0) == y, head, 0.0).astype(BF)
+    fr1[y] = fs1[...]
+    fresh_y = exchange(at_y, ny, y, lambda p: fs1, lambda me: fr1.at[me])
+    qt[...] = q_ref[...].T
     query_grad = SCALE * (wacc[...] / denom + less * positive)
     query_back = unit_back(raw, q_total, query_grad).astype(BF)
 
@@ -400,11 +405,6 @@
                 out_x[a, p, k].wait_recv()
                 hand_over(a, lax.rem(x + nx - k, nx), begin, size)
 
-    arrive(fresh_y)
-    fs2[...] = jnp.sum(fr1[...].astype(F32), axis=0).astype(BF)
-    fr2[z] = fs2[...]
-    fresh_z = exchange(at_z, nz, z, lambda p: fs2, lambda me: fr2.at[me])
-
     term[0] = dot(qt[...], query_back)
     c_q = core_send(0)
     arrive(c_q)
@@ -415,6 +415,12 @@
     br2[y] = bs2[y]
     back_y = exchange(at_y, ny, y, lambda p: bs2.at[p], lambda me: br2.at[me])
     y_send(0)
+    tt[...] = t_ref[...].T
+    arrive(fresh_y)
+    fs2[...] = jnp.sum(fr1[...].astype(F32), axis=0).astype(BF)
+    fr2[z] = fs2[...]
+    fresh_z = exchange(at_z, nz, z, lambda p: fs2, lambda me: fr2.at[me])
+    sems.drain()
     arrive(back_y)
     owned = dot(mt[...], br2[...].reshape(slots, -1))
     term[1] = split_dot(tt[...], owned)
@@ -427,6 +433,7 @@
     gather_x(0)
     z_i = z_send(1)
     gather_core(0)
+    sems.drain()
     arrive(fresh_z)
     fshape = (ns, nz * fs2.shape[0])
     want = lax.broadcasted_iota(jnp.int32, fshape, 0)
@@ -437,6 +444,7 @@
     gather_send(1, z_i)
     gather_x(1)
     gather_core(1)
+    sems.drain()
     arrive(to_core[1])
     sems.finish()
 

time: 99.1 us -> 98.5 us (level)
  no operation moved by 1% of the time
where the time goes in v4:
time: 98.5 us; the launch traced here: 98.3 us
  Pallas kernels  97.1 us (99%)
  between operations  1.29 us (1%)
    pallas_call x1, Pallas kernels, per_device(): pl.pallas_call(functools.partial(kernel, sizes), out_shape=[jax.ShapeDtyp...  94.5 us
    pallas_call x1, Pallas kernels, per_device(): pl.pallas_call(functools.partial(clip, nz), out_shape=[jax.ShapeDtypeStru...  2.53 us

profile of v4, /device:TPU:1, one launch (start us, length us, event | category | flops | bytes accessed | tf_op | source)
XLA Modules:
  0.0 98.3 jit_solution(7323730686774981818)
XLA Ops:
  1.3 94.5 %step.1 = (bf16[2,2,4,8,16,256]{5,4,3,2,1,0:T(8,128)(2,1)}, bf16[64,256]{1,0:T(8,128)(2,1)}) custom-call(bf16[512,1024]{1,0:T(8,128)(2,1)} %q_hbm.1, bf16[1024,256]{1,0:T(8,128)(2,1)} %qw_hbm.1, bf16[1024,256]{1,0:T(8,128)(2,1)} %iw_hbm.1, bf16[256,1024]{1,0:T(8,128)(2,1)} %t_hbm.1, bf16[128,256]{1,0:T(8,128)(2,1)} %queue_ref.1, s32[4,64]{1,0:T(4,128)} %bitcast.4, ...), custom_call_target="tpu_custom_call" | custom-call | tf_op jit(solution)/shard_map/step/pallas_call | solution.py:539
  95.8 2.5 %clip.1 = (bf16[2,4,8,16,256]{4,3,2,1,0:T(8,128)(2,1)}, bf16[2,4,8,16,256]{4,3,2,1,0:T(8,128)(2,1)}, bf16[128,256]{1,0:T(8,128)(2,1)}) custom-call(bf16[2,2,4,8,16,256]{5,4,3,2,1,0:T(8,128)(2,1)} %get-tuple-element.8.sums_ref, bf16[64,256]{1,0:T(8,128)(2,1)} %get-tuple-element.9.fresh_ref, bf16[128,256]{1,0:T(8,128)(2,1)} %queue_ref.1, s32[1]{0:T(128)S(6)} %copy.11.owner_ref), custom_call_target="tpu_custom_call" | custom-call | tf_op jit(solution)/shard_map/clip/pallas_call | solution.py:554
